TPU v7x, 32 devices: a whole 2x2x4 slice. The times are simulated.
32 devices in a mesh: dp: 8 (over y, x, core), seq: 4 (over z).
Axes of the slice: x: 2, y: 2, z: 4, core: 2. Of those that a mesh axis runs over, the one named last changes fastest.
Arguments:
- qkv_input: bfloat16 [4096, 3, 3072], P(('dp', 'seq')), may hold values from -40 to 40
- latents: bfloat16 [4096, 3072], P(('dp', 'seq')), may hold values from -0.29882812 to 0.29882812
- cotangent: bfloat16 [4096, 3072], P(('dp', 'seq')), may hold values from -6 to 6
- out_weight: bfloat16 [3072, 3072], P('seq', 'dp'), may hold values from -0.109375 to 0.109375
- gate_table: float32 [64, 3072], replicated, may hold values from -8 to 8
- timesteps: int32 [8, 3], P('dp'), may hold values from 0 to 63
- frames: int32 [8, 3], P('dp'), may hold values from 1 to 4, 8 in all within a row
Outputs:
- output: bfloat16 [4096, 3072], P(('dp', 'seq'))
- grad_qkv: bfloat16 [4096, 3, 3072], P(('dp', 'seq'))
- grad_weight: float32 [3072, 3072], P('seq', 'dp')
Inputs may be any that keep to these rules, and one draw needn't show every extreme that they name: Each pack's 3 clips cover its 8 frames exactly; in every pack the longest clip has 4 frames.
All inputs are finite; a program needn't handle non-finite values.
Results may differ from a plain program's by a relative error of at most 0.019.
Values may be sent and summed in bfloat16 or wider, within the bound.
A program may use at most 192 MiB of HBM per device.

v0:
```python
import jax
import jax.numpy as jnp
from jax import lax
from jax.sharding import PartitionSpec as P

HD = 128
FRAME_TOK = 64


def clip_index(frame_row, start, count):
    ends = jnp.cumsum(frame_row) * FRAME_TOK
    places = start + jnp.arange(count, dtype=jnp.int32)
    return jnp.sum((places[:, None] >= ends[None, :]).astype(jnp.int32), axis=1)


def token_gate(frame_row, step_row, table, start, count):
    bins = jnp.arange(table.shape[0], dtype=jnp.int32)
    pick = (step_row[:, None] == bins[None, :]).astype(jnp.float32)
    clip_rows = jnp.dot(pick, table, precision=lax.Precision.HIGHEST)
    which = clip_index(frame_row, start, count)
    member = (which[:, None] == jnp.arange(frame_row.shape[0], dtype=jnp.int32)[None, :]).astype(
        jnp.float32
    )
    return jnp.dot(member, clip_rows, precision=lax.Precision.HIGHEST)


def attend(query, keys, values, which):
    rows = query.shape[0]
    count = query.shape[1] // HD
    qf = query.reshape(rows, count, HD).astype(jnp.float32)
    kf = keys.reshape(rows, count, HD).astype(jnp.float32)
    vf = values.reshape(rows, count, HD).astype(jnp.float32)
    scores = jnp.einsum("qhd,khd->hqk", qf, kf) / jnp.sqrt(jnp.float32(HD))
    same = which[:, None] == which[None, :]
    scores = jnp.where(same[None], scores, jnp.float32(-1e30))
    top = jnp.max(scores, axis=-1, keepdims=True)
    expo = jnp.exp(scores - top)
    probs = expo / jnp.sum(expo, axis=-1, keepdims=True)
    probs_b = probs.astype(jnp.bfloat16)
    mixed = jnp.einsum("hqk,khd->qhd", probs_b.astype(jnp.float32), vf)
    return mixed.reshape(rows, count * HD)


def body(qkv_input, latents, cotangent, out_weight, gate_table, timesteps, frames):
    tok_rows = latents.shape[0]
    seq_count = lax.axis_size("seq")
    pack_rows = tok_rows * seq_count
    frame_row = frames[0]
    step_row = timesteps[0]
    heads = lax.all_to_all(qkv_input, "seq", split_axis=2, concat_axis=0, tiled=True)
    which = clip_index(frame_row, 0, pack_rows)
    attn_f, back = jax.vjp(
        lambda a, b, c: attend(a, b, c, which), heads[:, 0], heads[:, 1], heads[:, 2]
    )
    attn = attn_f.astype(jnp.bfloat16)
    w_rows = lax.all_gather(out_weight, "dp", axis=1, tiled=True)
    my_start = lax.axis_index("seq") * tok_rows
    gate_mine = token_gate(frame_row, step_row, gate_table, my_start, tok_rows)
    part = jnp.dot(attn, w_rows, preferred_element_type=jnp.float32).astype(jnp.bfloat16)
    part = lax.optimization_barrier(part)
    proj = lax.psum_scatter(
        part.astype(jnp.float32).astype(jnp.bfloat16), "seq", scatter_dimension=0, tiled=True
    ).astype(jnp.float32)
    output = (latents.astype(jnp.float32) + gate_mine * proj).astype(jnp.bfloat16)
    dproj = (gate_mine * cotangent.astype(jnp.float32)).astype(jnp.bfloat16)
    piece = lax.all_gather(dproj, "seq", axis=0, tiled=True)
    d_weight = jnp.einsum("th,td->hd", attn, piece, preferred_element_type=jnp.float32)
    update = jnp.einsum("td,hd->th", piece, w_rows, preferred_element_type=jnp.float32)
    d_attn = update
    d_attn, d_weight = (d_attn, d_weight)
    grad_weight = lax.psum_scatter(
        d_weight.astype(jnp.bfloat16), "dp", scatter_dimension=1, tiled=True
    ).astype(jnp.float32)
    rounded = lax.optimization_barrier(d_attn.astype(jnp.bfloat16))
    grad_q, grad_k, grad_v = back(rounded.astype(jnp.float32))
    grads = jnp.stack([grad_q, grad_k, grad_v], axis=1)
    grad_qkv = lax.all_to_all(grads, "seq", split_axis=0, concat_axis=2, tiled=True)
    return (output, grad_qkv, grad_weight)


def solution(mesh):
    placed = (
        P(("dp", "seq"), None, None),
        P(("dp", "seq"), None),
        P(("dp", "seq"), None),
        P("seq", "dp"),
        P(),
        P("dp", None),
        P("dp", None),
    )
    return jax.shard_map(
        body,
        mesh=mesh,
        in_specs=placed,
        out_specs=(P(("dp", "seq"), None), P(("dp", "seq"), None, None), P("seq", "dp")),
        check_vma=False,
    )
```

profile of v0, /device:TPU:16, one launch (start us, length us, event | category | flops | bytes accessed | tf_op | source)
XLA Modules:
  0.0 348.8 jit_solution(15093783001124139477)
XLA Ops:
  7.2 0.0 all-gather.5.cloned.1.call-start
  7.3 1.0 reduce-window.8
  8.2 0.1 convert_reduce_fusion.2
  8.3 1.0 fusion.21
  9.4 3.4 multiply_convert_fusion
  12.8 0.0 all-gather.5.cloned.1.call-update
  12.8 0.0 all-gather.3.cloned.1.call-start
  12.8 0.7 all-gather.3.cloned.1.call-update
  13.6 3.6 %copy.44 = bf16[128,3,3072]{0,1,2:T(4,128)(2,1)} copy(bf16[128,3,3072]{2,0,1:T(8,128)(2,1)S(1)} %copy-done.9) | data formatting | bytes 4718592 | tf_op args[0]
  17.2 5.2 %all-to-all-start = ((bf16[128,3,3072]{0,1,2:T(4,128)(2,1)}), bf16[128,3,3072]{0,1,2:T(4,128)(2,1)}, u32[]{:S(2)}, u32[]{:S(2)}) async-start(bf16[128,3,3072]{0,1,2:T(4,128)(2,1)} %copy.44), calls=%async_computation | async-start | bytes 6291456 | tf_op jit(solution)/shard_map/all_to_all | solution.py:50
  22.4 0.1 convert_reduce_fusion.1
  22.5 0.2 broadcast_compare_fusion
  22.7 117.7 %all-to-all-done = bf16[128,3,3072]{0,1,2:T(4,128)(2,1)} async-done(((bf16[128,3,3072]{0,1,2:T(4,128)(2,1)}), bf16[128,3,3072]{0,1,2:T(4,128)(2,1)}, u32[]{:S(2)}, u32[]{:S(2)}) %all-to-all-start) | async-done | bytes 2359328 | tf_op jit(solution)/shard_map/all_to_all | solution.py:50
  140.4 5.5 %copy.68 = bf16[128,3,4,768]{0,2,3,1:T(4,128)(2,1)} copy(bf16[128,3,4,768]{0,1,3,2:T(4,128)(2,1)} %bitcast.3) | data formatting | bytes 4718592 | tf_op jit(solution)/shard_map/all_to_all | solution.py:50
  145.9 4.0 %all_to_all.29 = bf16[512,3,768]{0,2,1:T(8,128)(2,1)S(1)} reshape(bf16[4,128,3,768]{1,0,3,2:T(4,128)(2,1)} %bitcast.57) | data formatting | bytes 4718592 | tf_op jit(solution)/shard_map/all_to_all | solution.py:50
  149.9 1.0 fusion.30
  151.0 0.9 copy-done.6
  151.9 1.3 fusion.5
  153.2 2.6 copy-done.2
  155.9 1.3 fusion.16
  157.2 0.0 all-gather.5.cloned.1.call-done
  157.2 19.1 %all-gather.3.cloned.1.call-done = bf16[768,3072]{1,0:T(8,128)(2,1)} async-done(((bf16[768,384]{1,0:T(8,128)(2,1)}), bf16[768,3072]{1,0:T(8,128)(2,1)}) %all-gather.3.cloned.1.call-update) | async-done | bytes 4718608 | tf_op jit(solution)/shard_map/all_gather | solution.py:56
  176.4 6.8 %convolution_convert_fusion.5 = bf16[512,768]{1,0:T(8,128)(2,1)} fusion(bf16[512,3072]{1,0:T(8,128)(2,1)} %all-gather.5.cloned.1.call-done, bf16[768,3072]{1,0:T(8,128)(2,1)} %all-gather.3.cloned.1.call-done), kind=kOutput, calls=%fused_computation.35 | convolution fusion | flops 2416312320 | bytes 8650752 | tf_op jit(solution)/shard_map/td,hd->th/dot_general | solution.py:68
  183.2 2.5 copy.49
  185.7 8.0 %convert_reduce_fusion = (f32[6,512]{1,0:T(8,128)S(1)}, pred[6,512,512]{1,2,0:T(32,128)(4,1)}, f32[6,512]{1,0:T(8,128)S(1)}, bf16[6,512,512]{1,2,0:T(8,128)(2,1)S(1)}) fusion(f32[6,512]{1,0:T(8,128)S(1)} %get-tuple-element.12, f32[6,512,512]{1,2,0:T(8,128)} %copy-done.2, pred[512,512]{0,1:T(8,128)(4,1)S(1)} %broadcast_compare_fusion, ...), kind=kOutput, calls=%fused_computation.7 | convolution fusion | flops 419948544 | bytes 12894208 | tf_op jit(solution)/shard_map/transpose(jvp(hqk,khd->qhd))/dot_general | solution.py:40
  193.7 4.4 %fusion.27 = (f32[6,512]{1,0:T(8,128)S(1)}, f32[6,512,512]{1,2,0:T(8,128)}, bf16[6,512,512]{1,2,0:T(8,128)(2,1)S(1)}) fusion(f32[6,512]{1,0:T(8,128)S(1)} %get-tuple-element.12, f32[6,512,512]{1,2,0:T(8,128)S(1)} %bitcast.54, pred[512,512]{0,1:T(8,128)(4,1)S(1)} %broadcast_compare_fusion, f32[6,512]{1,0:T(8,128)S(1)} %neg.9, f32[6,512]{1,0:T(8,128)S(1)} %fusion.16, ...), kind=kLoop, calls=%fused_computation.54 | loop fusion | flops 15725568 | bytes 19185664 | tf_op jit(solution)/shard_map/transpose(jvp())/reduce_sum | solution.py:37
  198.1 1.7 copy-done.3
  199.7 0.6 convolution_convert_fusion.3
  200.3 6.6 %convolution_convert_fusion.1 = bf16[512,3072]{1,0:T(8,128)(2,1)} fusion(bf16[512,768]{0,1:T(8,128)(2,1)S(1)} %bitcast.67, bf16[768,3072]{1,0:T(8,128)(2,1)} %all-gather.3.cloned.1.call-done), kind=kOutput, calls=%fused_computation.14 | convolution fusion | flops 2417491968 | bytes 8650752 | tf_op jit(solution)/shard_map/dot_general | solution.py:59
  206.9 0.0 reduce-scatter.5.cloned.1.call-update
  206.9 0.0 reduce-scatter.7.cloned.1.call-start
  207.0 6.1 %convolution_convert_fusion = bf16[768,3072]{1,0:T(8,128)(2,1)} fusion(bf16[512,768]{0,1:T(8,128)(2,1)S(1)} %bitcast.68, bf16[512,3072]{1,0:T(8,128)(2,1)} %all-gather.5.cloned.1.call-done), kind=kOutput, calls=%fused_computation.11 | convolution fusion | flops 2418278400 | bytes 8650752 | tf_op jit(solution)/shard_map/th,td->hd/dot_general | solution.py:67
  213.1 6.9 %copy.65 = bf16[768,3072]{0,1:T(8,128)(2,1)} copy(bf16[768,3072]{1,0:T(8,128)(2,1)} %convolution_convert_fusion) | data formatting | bytes 9437184
  220.0 0.0 reduce-scatter.7.cloned.1.call-update
  220.0 1.1 copy-done.5
  221.1 3.0 convolution_convert_fusion.4
  224.2 1.6 copy.56
  225.8 6.3 %fusion.18 = bf16[6,512,128]{1,2,0:T(8,128)(2,1)} fusion(bf16[512,6,128]{0,2,1:T(8,128)(2,1)} %bitcast.66, f32[6,512,512]{1,2,0:T(8,128)} %get-tuple-element.4, pred[6,512,512]{1,2,0:T(32,128)(4,1)} %get-tuple-element.6, f32[6,512]{1,0:T(8,128)S(1)} %negate_divide_fusion, pred[512,512]{0,1:T(8,128)(4,1)S(1)} %broadcast_compare_fusion), kind=kOutput, calls=%fused_computation.32 | convolution fusion | flops 409337856 | bytes 9711616 | tf_op jit(solution)/shard_map/transpose(jvp(qhd,khd->hqk))/dot_general | solution.py:33
  232.1 4.8 %copy.55 = bf16[512,1,768]{2,1,0:T(2,128)(2,1)} copy(bf16[512,1,768]{0,2,1:T(8,128)(2,1)} %bitcast.70) | data formatting | bytes 1572864 | tf_op jit(solution)/shard_map/stack;transpose(jvp())/reshape | solution.py:76
  236.9 6.0 %fusion.17 = bf16[6,512,128]{1,2,0:T(8,128)(2,1)} fusion(bf16[512,6,128]{0,2,1:T(8,128)(2,1)S(1)} %bitcast.64, f32[6,512,512]{1,2,0:T(8,128)} %get-tuple-element.4, pred[6,512,512]{1,2,0:T(32,128)(4,1)} %get-tuple-element.6, f32[6,512]{1,0:T(8,128)S(1)} %negate_divide_fusion, pred[512,512]{0,1:T(8,128)(4,1)S(1)} %broadcast_compare_fusion), kind=kOutput, calls=%fused_computation.31 | convolution fusion | flops 409337856 | bytes 9711616 | tf_op jit(solution)/shard_map/transpose(jvp(qhd,khd->hqk))/dot_general | solution.py:33
  242.9 4.8 %copy.54 = bf16[512,1,768]{2,1,0:T(2,128)(2,1)} copy(bf16[512,1,768]{0,2,1:T(8,128)(2,1)} %bitcast.69) | data formatting | bytes 1572864 | tf_op jit(solution)/shard_map/stack;transpose(jvp())/reshape | solution.py:76
  247.7 6.7 %pad_maximum_fusion = bf16[512,3,768]{2,1,0:T(4,128)(2,1)S(1)} fusion(bf16[512,1,768]{2,1,0:T(2,128)(2,1)S(1)} %copy.56, bf16[512,1,768]{2,1,0:T(2,128)(2,1)} %copy.55, bf16[512,1,768]{2,1,0:T(2,128)(2,1)} %copy.54), kind=kLoop, calls=%fused_computation.17 | loop fusion | flops 7077888 | bytes 4718592 | tf_op jit(solution)/shard_map/stack | solution.py:76
  254.4 77.2 %all_to_all.36 = bf16[512,3,768]{2,1,0:T(4,128)(2,1)S(1)} all-to-all(bf16[512,3,768]{2,1,0:T(4,128)(2,1)S(1)} %pad_maximum_fusion), channel_id=1, replica_groups=mesh['dp'=8,'seq'=4] {'seq'}, dimensions={0} | all-to-all | bytes 4718592 | tf_op jit(solution)/shard_map/all_to_all | solution.py:77
  331.6 2.2 copy.57
  333.9 2.9 all_to_all.33
  336.8 3.0 add_convert_fusion
  339.8 1.4 copy.66
  341.2 1.1 convert_element_type.104
  (29 shorter events, 0.1 us)
Async XLA Ops:
  7.2 1.2 copy-start
  7.2 6.4 %copy-start.9 = (bf16[128,3,3072]{2,0,1:T(8,128)(2,1)S(1)}, bf16[128,3,3072]{2,0,1:T(8,128)(2,1)}, u32[]{:S(2)}) copy-start(bf16[128,3,3072]{2,0,1:T(8,128)(2,1)} %param.7) | copy-start | bytes 7077892
  7.2 150.0 %all-gather.5.cloned.1.call-start = ((), (), s32[]{:S(2)}) async-start(), calls=%async_computation.6 | async-start | bytes 3932160 | tf_op jit(solution)/shard_map/all_gather | solution.py:66
  12.8 163.6 %all-gather.3.cloned.1.call-start = ((), (), s32[]{:S(2)}) async-start(), calls=%async_computation.4 | async-start | bytes 5308416 | tf_op jit(solution)/shard_map/all_gather | solution.py:56
  17.2 123.2 %all-to-all-start = ((bf16[128,3,3072]{0,1,2:T(4,128)(2,1)}), bf16[128,3,3072]{0,1,2:T(4,128)(2,1)}, u32[]{:S(2)}, u32[]{:S(2)}) async-start(bf16[128,3,3072]{0,1,2:T(4,128)(2,1)} %copy.44), calls=%async_computation | async-start | bytes 6291456 | tf_op jit(solution)/shard_map/all_to_all | solution.py:50
  22.4 314.4 %reduce-scatter.5.cloned.1.call-start = ((), (), s32[]{:S(2)}) async-start(), calls=%async_computation.5 | async-start | bytes 3932160 | tf_op jit(solution)/shard_map/reduce_scatter | solution.py:61
  151.0 0.9 copy-start.6
  151.0 2.2 copy-start.8
  153.2 2.6 copy-start.2
  183.2 10.5 %slice-start = ((s8[6291456]{0:T(1024)(128)(4,1)}), s8[2097152]{0:T(1024)(128)(4,1)S(1)}, s32[]{:S(2)}) async-start(s8[6291456]{0:T(1024)(128)(4,1)} %bitcast.53), calls=%async_computation.8 | async-start | bytes 4194304
  185.7 8.0 %slice-start.1 = ((s8[6291456]{0:T(1024)(128)(4,1)}), s8[4194304]{0:T(1024)(128)(4,1)S(1)}, s32[]{:S(2)}) async-start(s8[6291456]{0:T(1024)(128)(4,1)} %bitcast.53), calls=%async_computation.9 | async-start | bytes 8388608
  193.7 6.0 %copy-start.4 = (bf16[512,1,768]{0,2,1:T(8,128)(2,1)S(1)}, bf16[512,1,768]{0,2,1:T(8,128)(2,1)}, u32[]{:S(2)}) copy-start(bf16[512,1,768]{0,2,1:T(8,128)(2,1)} %get-tuple-element.10) | copy-start | bytes 2359300
  198.1 1.7 copy-start.3
  206.9 132.9 %reduce-scatter.7.cloned.1.call-start = ((), (), s32[]{:S(2)}) async-start(), calls=%async_computation.7 | async-start | bytes 5308416
  220.0 1.2 copy-start.5
  225.8 11.1 %copy-start.7 = (bf16[512,1,768]{0,2,1:T(8,128)(2,1)S(1)}, bf16[512,1,768]{0,2,1:T(8,128)(2,1)}, u32[]{:S(2)}) copy-start(bf16[512,1,768]{0,2,1:T(8,128)(2,1)} %copy-done.6) | copy-start | bytes 2359300
  331.6 10.6 %copy-start.1 = (f32[64,3072]{1,0:T(8,128)S(1)}, f32[64,3072]{1,0:T(8,128)}, u32[]{:S(2)}) copy-start(f32[64,3072]{1,0:T(8,128)} %param.11) | copy-start | bytes 2359300
Sparse Core Ops, SparseCore 0:
  12.9 119.9 all-gather.4
  134.8 41.5 all-gather.2
  207.0 64.5 reduce-scatter.4
  274.9 55.2 reduce-scatter.6
where the time goes:
time: 354 us; the launch traced here: 349 us
  waiting for transfers between devices  138 us (39%)
  blocking collectives  77.2 us (22%)
  matrix products  49.2 us (14%)
  local copies, waits for them, and re-layouts  47.6 us (13%)
  other arithmetic  17.9 us (5%)
  between operations  13.9 us (4%)
  starting transfers between devices  5.33 us (2%)
    all_to_all x1, waiting for transfers between devices, body(): lax.all_to_all(qkv_input, 'seq', split_axis=2, concat_axis=0, tiled=True)  118 us
    all_to_all x1, blocking collectives, body(): lax.all_to_all(grads, 'seq', split_axis=0, concat_axis=2, tiled=True)  77.2 us
    all_gather x1, waiting for transfers between devices, body(): w_rows = lax.all_gather(out_weight, 'dp', axis=1, tiled=True)  19.1 us
    unnamed x27, local copies, waits for them, and re-layouts  18.3 us
    dot_general x3, matrix products, attend(): scores = jnp.einsum('qhd,khd->hqk', qf, kf) / jnp.sqrt(jnp.float32(HD))  13.6 us
    dot_general x3, matrix products, attend(): mixed = jnp.einsum('hqk,khd->qhd', probs_b.astype(jnp.float32), vf)  11.6 us
    reshape x3, local copies, waits for them, and re-layouts, body(): grads = jnp.stack([grad_q, grad_k, grad_v], axis=1)  11.2 us
    all_to_all x2, local copies, waits for them, and re-layouts, body(): lax.all_to_all(qkv_input, 'seq', split_axis=2, concat_axis=0, tiled=True)  9.56 us
  transfers between devices with their start and end apart: 5, of which 2 were waited for; matrix products, arithmetic and copies ran while one was open for 19% of the time, Pallas kernels for 0%

commit v1 on v0

v1 whole, which is shorter than its diff:
```python
import functools

import jax
import jax.numpy as jnp
from jax import lax
from jax.experimental import pallas as pl
from jax.experimental.pallas import tpu as pltpu
from jax.sharding import PartitionSpec as P

HD = 128
FRAME_TOK = 64
QUERY_TILE = 256
MESH = pl.DeviceIdType.MESH
TRANSPOSED_RHS = (((1,), (1,)), ((), ()))
TRANSPOSED_LHS = (((0,), (0,)), ((), ()))


def dot(a, b, dims=(((1,), (0,)), ((), ()))):
    return lax.dot_general(a, b, dims, preferred_element_type=jnp.float32)


def greet(n, dp, me):
    barrier = pltpu.get_barrier_semaphore()
    for k in range(1, n):
        pl.semaphore_signal(barrier, inc=1, device_id=(dp, lax.rem(me + k, n)), device_id_type=MESH)
    pl.semaphore_wait(barrier, n - 1)


def clip_of(frames_ref, places):
    end = 0
    which = jnp.zeros_like(places)
    for c in range(frames_ref.shape[1] - 1):
        end = end + frames_ref[0, c] * FRAME_TOK
        which = which + (places >= end).astype(jnp.int32)
    return which


def gate_rows(table_ref, steps_ref, frames_ref, start, count):
    places = start + lax.broadcasted_iota(jnp.int32, (count, 1), 0)
    which = clip_of(frames_ref, places)
    gate = table_ref[pl.ds(steps_ref[0, 0], 1), :]
    for c in range(1, steps_ref.shape[1]):
        gate = jnp.where(which >= c, table_ref[pl.ds(steps_ref[0, c], 1), :], gate)
    return gate


def probabilities(q, k, frames_ref, start, rows):
    count = q.shape[0]
    scores = dot(q, k, TRANSPOSED_RHS) * jnp.float32(HD ** -0.5)
    mine = clip_of(frames_ref, start + lax.broadcasted_iota(jnp.int32, (count, 1), 0))
    theirs = clip_of(frames_ref, lax.broadcasted_iota(jnp.int32, (1, rows), 1))
    scores = jnp.where(mine == theirs, scores, jnp.float32(-1e30))
    expo = jnp.exp(scores - jnp.max(scores, axis=-1, keepdims=True))
    return expo * (1.0 / jnp.sum(expo, axis=-1, keepdims=True))


def gather_kernel(
    n, qkv_ref, cot_ref, table_ref, steps_ref, frames_ref,
    heads_ref, attn_ref, piece_ref, dw_ref,
    flipped, own_sem, qs_sem, qr_sem, gs_sem, gr_sem,
):
    me = lax.axis_index("seq")
    dp = lax.axis_index("dp")
    group, _, rows, _ = heads_ref.shape
    tok = rows // n
    wide = dw_ref.shape[1]
    tile = min(QUERY_TILE, rows)

    def slab(block):
        return pl.ds(pl.multiple_of(block * tok, tok), tok)

    def block_copy(side, block):
        to = me + 1 if side == 0 else me - 1
        return pltpu.make_async_remote_copy(
            src_ref=piece_ref.at[slab(block), :],
            dst_ref=piece_ref.at[slab(block), :],
            send_sem=gs_sem.at[side, block],
            recv_sem=gr_sem.at[side, block],
            device_id=(dp, to),
            device_id_type=MESH,
        )

    def head_copy(k, h):
        peer = lax.rem(me + k, n)
        return pltpu.make_async_remote_copy(
            src_ref=qkv_ref.at[peer * group + h],
            dst_ref=heads_ref.at[h, :, slab(me), :],
            send_sem=qs_sem.at[k - 1, h],
            recv_sem=qr_sem.at[k - 1, h],
            device_id=(dp, peer),
            device_id_type=MESH,
        )

    def head_landed(k, h):
        source = lax.rem(me + n - k, n)
        pltpu.make_async_remote_copy(
            src_ref=qkv_ref.at[h],
            dst_ref=heads_ref.at[h, :, slab(source), :],
            send_sem=qs_sem.at[k - 1, h],
            recv_sem=qr_sem.at[k - 1, h],
            device_id=(dp, source),
            device_id_type=MESH,
        ).wait_recv()

    greet(n, dp, me)
    own = pltpu.make_async_copy(
        qkv_ref.at[pl.ds(me * group, group)], heads_ref.at[:, :, slab(me), :], own_sem
    )
    own.start()

    @pl.loop(0, group)
    def _(h):
        for k in range(1, n):
            head_copy(k, h).start()

    gate = gate_rows(table_ref, steps_ref, frames_ref, me * tok, tok)
    piece_ref[slab(me), :] = (gate * cot_ref[...].astype(jnp.float32)).astype(jnp.bfloat16)

    @pl.when(me < n - 1)
    def _():
        block_copy(0, me).start()

    @pl.when(me > 0)
    def _():
        block_copy(1, me).start()

    own.wait()

    def forward(h):
        for k in range(1, n):
            head_landed(k, h)

        @pl.loop(0, rows // tile)
        def _(t):
            here = pl.ds(pl.multiple_of(t * tile, tile), tile)
            probs = probabilities(
                heads_ref[h, 0, here, :], heads_ref[h, 1], frames_ref, t * tile, rows
            )
            mixed = dot(probs.astype(jnp.bfloat16), heads_ref[h, 2])
            attn_ref[here, pl.ds(pl.multiple_of(h * HD, HD), HD)] = mixed.astype(jnp.bfloat16)

    for s in range(1, n):
        @pl.when(me - s >= 0)
        def _():
            block_copy(0, me - s).wait_recv()

            @pl.when(me < n - 1)
            def _():
                block_copy(0, me - s).start()

        @pl.when(me + s < n)
        def _():
            block_copy(1, me + s).wait_recv()

            @pl.when(me > 0)
            def _():
                block_copy(1, me + s).start()

        pl.loop((s - 1) * group // (n - 1), s * group // (n - 1))(forward)

    flipped[...] = attn_ref[...].T
    step = 512

    @pl.loop(0, wide // step)
    def _(c):
        cols = pl.ds(pl.multiple_of(c * step, step), step)
        dw_ref[:, cols] = dot(flipped[...], piece_ref[:, cols]).astype(jnp.bfloat16)

    @pl.loop(0, group)
    def _(h):
        for k in range(1, n):
            head_copy(k, h).wait_send()

    for s in range(0, n):
        @pl.when((me - s >= 0) & (me < n - 1))
        def _():
            block_copy(0, me - s).wait_send()

        @pl.when((me + s < n) & (me > 0))
        def _():
            block_copy(1, me + s).wait_send()


def scatter_kernel(
    n, heads_ref, attn_ref, piece_ref, w_ref, lat_ref, table_ref, steps_ref, frames_ref,
    out_ref, grads_ref,
    part, landed, dattn, gbuf, own_sem, ps_sem, pr_sem, hs_sem, hr_sem,
):
    me = lax.axis_index("seq")
    dp = lax.axis_index("dp")
    group, _, rows, _ = heads_ref.shape
    tok = rows // n
    wide = w_ref.shape[1]
    tile = min(QUERY_TILE, rows)

    def slab(block):
        return pl.ds(pl.multiple_of(block * tok, tok), tok)

    def sum_copy(side, block):
        to = me + 1 if side == 0 else me - 1
        return pltpu.make_async_remote_copy(
            src_ref=part.at[block],
            dst_ref=landed.at[side, block],
            send_sem=ps_sem.at[side, block],
            recv_sem=pr_sem.at[side, block],
            device_id=(dp, to),
            device_id_type=MESH,
        )

    def grad_copy(k, h):
        peer = lax.rem(me + k, n)
        return pltpu.make_async_remote_copy(
            src_ref=gbuf.at[h, :, slab(peer), :],
            dst_ref=grads_ref.at[me * group + h],
            send_sem=hs_sem.at[k - 1, h],
            recv_sem=hr_sem.at[k - 1, h],
            device_id=(dp, peer),
            device_id_type=MESH,
        )

    def grad_landed(k, h):
        source = lax.rem(me + n - k, n)
        pltpu.make_async_remote_copy(
            src_ref=gbuf.at[h, :, slab(source), :],
            dst_ref=grads_ref.at[source * group + h],
            send_sem=hs_sem.at[k - 1, h],
            recv_sem=hr_sem.at[k - 1, h],
            device_id=(dp, source),
            device_id_type=MESH,
        ).wait_recv()

    def own_copy(h):
        return pltpu.make_async_copy(
            gbuf.at[h, :, slab(me), :], grads_ref.at[me * group + h], own_sem.at[h]
        )

    greet(n, dp, me)
    step = 512

    def project(block):
        @pl.loop(0, wide // step)
        def _(c):
            cols = pl.ds(pl.multiple_of(c * step, step), step)
            part[block, :, cols] = dot(attn_ref[slab(block), :], w_ref[:, cols]).astype(
                jnp.bfloat16
            )

    def relay(side, block):
        sum_copy(side, block).wait_recv()

        @pl.loop(0, tok // 16)
        def _(r):
            here = pl.ds(pl.multiple_of(r * 16, 16), 16)
            part[block, here, :] = (
                part[block, here, :].astype(jnp.float32)
                + landed[side, block, here, :].astype(jnp.float32)
            ).astype(jnp.bfloat16)

        sum_copy(side, block).start()

    for s in range(n - 1, -1, -1):
        @pl.when(me + s < n)
        def _():
            project(me + s)
            if s > 0:
                @pl.when(me == 0)
                def _():
                    sum_copy(0, me + s).start()

        if s > 0:
            @pl.when(me - s >= 0)
            def _():
                project(me - s)

                @pl.when(me == n - 1)
                def _():
                    sum_copy(1, me - s).start()

    head_cols = 2 * HD if (group * HD) % (2 * HD) == 0 else HD
    for c in range(0, group * HD, head_cols):
        dattn[:, c:c + head_cols] = dot(
            piece_ref[...], w_ref[c:c + head_cols, :], TRANSPOSED_RHS
        ).astype(jnp.bfloat16)

    def backward(h):
        q_cols = pl.ds(pl.multiple_of(h * HD, HD), HD)
        grad_k = jnp.zeros((rows, HD), jnp.float32)
        grad_v = jnp.zeros((rows, HD), jnp.float32)
        for t in range(rows // tile):
            here = slice(t * tile, (t + 1) * tile)
            q, keys = heads_ref[h, 0, here, :], heads_ref[h, 1]
            probs = probabilities(q, keys, frames_ref, t * tile, rows)
            up = dattn[here, q_cols]
            dprobs = dot(up, heads_ref[h, 2], TRANSPOSED_RHS)
            dprobs = dprobs.astype(jnp.bfloat16).astype(jnp.float32)
            dscores = probs * (dprobs - jnp.sum(probs * dprobs, axis=-1, keepdims=True))
            dscores = (dscores * jnp.float32(HD ** -0.5)).astype(jnp.bfloat16)
            gbuf[h, 0, here, :] = dot(dscores, keys).astype(jnp.bfloat16)
            grad_k = grad_k + dot(dscores, q, TRANSPOSED_LHS)
            grad_v = grad_v + dot(probs.astype(jnp.bfloat16), up, TRANSPOSED_LHS)
        gbuf[h, 1] = grad_k.astype(jnp.bfloat16)
        gbuf[h, 2] = grad_v.astype(jnp.bfloat16)
        for k in range(1, n):
            grad_copy(k, h).start()
        own_copy(h).start()

    for s in range(1, n):
        pl.loop((s - 1) * group // (n - 1), s * group // (n - 1))(backward)

        @pl.when((n - s > me) & (me > 0))
        def _():
            relay(0, n - s)

        @pl.when((s - 1 < me) & (me < n - 1))
        def _():
            relay(1, s - 1)

    @pl.when(me > 0)
    def _():
        sum_copy(0, me).wait_recv()

    @pl.when(me == 0)
    def _():
        landed[0, 0] = jnp.zeros_like(landed[0, 0])

    @pl.when(me < n - 1)
    def _():
        sum_copy(1, me).wait_recv()

    @pl.when(me == n - 1)
    def _():
        landed[1, n - 1] = jnp.zeros_like(landed[1, n - 1])

    gate = gate_rows(table_ref, steps_ref, frames_ref, me * tok, tok)
    proj = (
        part[me].astype(jnp.float32)
        + landed[0, me].astype(jnp.float32)
        + landed[1, me].astype(jnp.float32)
    )
    out_ref[...] = (lat_ref[...].astype(jnp.float32) + gate * proj).astype(jnp.bfloat16)

    for s in range(1, n):
        @pl.when(me + s < n)
        def _():
            sum_copy(0, me + s).wait_send()

        @pl.when(me - s >= 0)
        def _():
            sum_copy(1, me - s).wait_send()

    @pl.loop(0, group)
    def _(h):
        own_copy(h).wait()
        for k in range(1, n):
            grad_landed(k, h)
            grad_copy(k, h).wait_send()


def body(qkv_input, latents, cotangent, out_weight, gate_table, timesteps, frames):
    tok, wide = latents.shape
    n = lax.axis_size("seq")
    rows = tok * n
    heads = wide // HD
    group = heads // n
    bf16 = jnp.bfloat16
    vmem = pl.BlockSpec(memory_space=pltpu.VMEM)
    smem = pl.BlockSpec(memory_space=pltpu.SMEM)
    anyspace = pl.BlockSpec(memory_space=pl.ANY)
    dma = pltpu.SemaphoreType.DMA

    w_rows = lax.all_gather(out_weight, "dp", axis=1, tiled=True)
    by_head = qkv_input.reshape(tok, 3, heads, HD).transpose(2, 1, 0, 3)
    flops = 2 * rows * wide * group * HD
    packed, attn, piece, d_weight = pl.pallas_call(
        functools.partial(gather_kernel, n),
        out_shape=(
            jax.ShapeDtypeStruct((group, 3, rows, HD), bf16),
            jax.ShapeDtypeStruct((rows, group * HD), bf16),
            jax.ShapeDtypeStruct((rows, wide), bf16),
            jax.ShapeDtypeStruct((group * HD, wide), bf16),
        ),
        in_specs=[anyspace, vmem, vmem, smem, smem],
        out_specs=(vmem, vmem, vmem, vmem),
        scratch_shapes=[
            pltpu.VMEM((group * HD, rows), bf16),
            dma,
            dma((n - 1, group)),
            dma((n - 1, group)),
            dma((2, n)),
            dma((2, n)),
        ],
        compiler_params=pltpu.CompilerParams(
            collective_id=0, has_side_effects=True, vmem_limit_bytes=40 * 2**20
        ),
        cost_estimate=pl.CostEstimate(
            flops=20 * flops, bytes_accessed=200 * 2**20, transcendentals=0
        ),
        name="gather_and_attend",
    )(by_head, cotangent, gate_table, timesteps, frames)

    grad_weight = lax.psum_scatter(d_weight, "dp", scatter_dimension=1, tiled=True)

    output, grads = pl.pallas_call(
        functools.partial(scatter_kernel, n),
        out_shape=(
            jax.ShapeDtypeStruct((tok, wide), bf16),
            jax.ShapeDtypeStruct((heads, 3, tok, HD), bf16),
        ),
        in_specs=[vmem, vmem, vmem, vmem, vmem, vmem, smem, smem],
        out_specs=(vmem, anyspace),
        scratch_shapes=[
            pltpu.VMEM((n, tok, wide), bf16),
            pltpu.VMEM((2, n, tok, wide), bf16),
            pltpu.VMEM((rows, group * HD), bf16),
            pltpu.VMEM((group, 3, rows, HD), bf16),
            dma((group,)),
            dma((2, n)),
            dma((2, n)),
            dma((n - 1, group)),
            dma((n - 1, group)),
        ],
        compiler_params=pltpu.CompilerParams(
            collective_id=1, has_side_effects=True, vmem_limit_bytes=56 * 2**20
        ),
        cost_estimate=pl.CostEstimate(
            flops=20 * flops, bytes_accessed=200 * 2**20, transcendentals=0
        ),
        name="project_and_scatter",
    )(packed, attn, piece, w_rows, latents, gate_table, timesteps, frames)

    grad_qkv = grads.transpose(2, 1, 0, 3).reshape(tok, 3, wide)
    return output, grad_qkv, grad_weight.astype(jnp.float32)


def solution(mesh):
    placed = (
        P(("dp", "seq"), None, None),
        P(("dp", "seq"), None),
        P(("dp", "seq"), None),
        P("seq", "dp"),
        P(),
        P("dp", None),
        P("dp", None),
    )
    return jax.shard_map(
        body,
        mesh=mesh,
        in_specs=placed,
        out_specs=(P(("dp", "seq"), None), P(("dp", "seq"), None, None), P("seq", "dp")),
        check_vma=False,
    )
```

time: 354 us -> 377 us (1.065)
  Pallas kernels: 0 us -> 231 us
  blocking collectives: 77.2 us -> 0 us
  matrix products: 49.2 us -> 0 us
  waiting for transfers between devices: 138 us -> 101 us
  local copies, waits for them, and re-layouts: 47.6 us -> 26.9 us
  other arithmetic: 17.9 us -> 1.09 us
  starting transfers between devices: 5.33 us -> 0.08 us
    pallas_call x0 -> x2, Pallas kernels: none -> 231 us  [the longest x1 124 us: body(): pl.pallas_call(functools.partial(scatter_kernel, n), out_shape=(jax.Shape...]
    all_to_all x1 -> x0, waiting for transfers between devices: 118 us -> none  [body(): lax.all_to_all(qkv_input, 'seq', split_axis=2, concat_axis=0, tiled=True)]
    all_to_all x1 -> x0, blocking collectives: 77.2 us -> none  [body(): lax.all_to_all(grads, 'seq', split_axis=0, concat_axis=2, tiled=True)]
    unnamed x5 -> x3, waiting for transfers between devices: 0.75 us -> 62.1 us
    dot_general x11 -> x0, matrix products: 49.2 us -> none  [the longest x3 13.6 us: attend(): scores = jnp.einsum('qhd,khd->hqk', qf, kf) / jnp.sqrt(jnp.float32(HD))]
    all_gather x1, waiting for transfers between devices: 19.1 us -> 39.3 us  [body(): w_rows = lax.all_gather(out_weight, 'dp', axis=1, tiled=True)]
    all_to_all x4 -> x0, local copies, waits for them, and re-layouts: 14.7 us -> none  [the longest x2 9.56 us: body(): lax.all_to_all(qkv_input, 'seq', split_axis=2, concat_axis=0, tiled=True)]
    reshape x3 -> x1, local copies, waits for them, and re-layouts: 11.2 us -> 3.12 us  [body(): by_head = qkv_input.reshape(tok, 3, heads, HD).transpose(2, 1, 0, 3)]
  transfers between devices with their start and end apart: 5 -> 2, of which waited for: 2 -> 2; matrix products, arithmetic and copies ran while one was open for 19% -> 1% of each run, Pallas kernels for 0% -> 0%
where the time goes in v1:
time: 377 us; the launch traced here: 375 us
  Pallas kernels  231 us (61%)
  waiting for transfers between devices  101 us (27%)
  local copies, waits for them, and re-layouts  26.9 us (7%)
  between operations  14.1 us (4%)
    pallas_call x1, Pallas kernels, body(): pl.pallas_call(functools.partial(scatter_kernel, n), out_shape=(jax.Shape...  124 us
    pallas_call x1, Pallas kernels, body(): pl.pallas_call(functools.partial(gather_kernel, n), out_shape=(jax.ShapeD...  107 us
    unnamed x3, waiting for transfers between devices  62.1 us
    all_gather x1, waiting for transfers between devices, body(): w_rows = lax.all_gather(out_weight, 'dp', axis=1, tiled=True)  39.3 us
    unnamed x21, local copies, waits for them, and re-layouts  20.8 us
  transfers between devices with their start and end apart: 2, of which 2 were waited for; matrix products, arithmetic and copies ran while one was open for 1% of the time, Pallas kernels for 0%

profile of v1, /device:TPU:16, one launch (start us, length us, event | category | flops | bytes accessed | tf_op | source)
XLA Modules:
  0.0 374.5 jit_solution(15051880602930302146)
XLA Ops:
  7.2 0.0 reduce-scatter.4.cloned.1.call-start
  7.2 4.3 %copy.14 = bf16[128,3,3072]{0,2,1:T(8,128)(2,1)} copy(bf16[128,3,3072]{2,0,1:T(8,128)(2,1)} %param.7) | data formatting | bytes 4718592 | tf_op args[0]
  11.5 0.0 copy-start
  11.5 0.0 copy-start.2
  11.5 0.0 copy-start.3
  11.5 3.1 copy.15
  14.6 0.0 copy-done
  14.6 0.0 copy-done.2
  14.6 0.0 copy-done.3
  14.6 0.0 copy-start.1
  14.7 1.1 copy-done.1
  15.8 107.1 %gather_and_attend.1 = (bf16[6,3,512,128]{3,2,1,0:T(8,128)(2,1)S(1)}, bf16[512,768]{1,0:T(8,128)(2,1)S(1)}, bf16[512,3072]{1,0:T(8,128)(2,1)S(1)}, bf16[768,3072]{1,0:T(8,128)(2,1)}) custom-call(bf16[24,3,128,128]{3,2,1,0:T(8,128)(2,1)S(1)} %bitcast.6, bf16[128,3072]{1,0:T(8,128)(2,1)S(1)} %copy-done, f32[64,3072]{1,0:T(8,128)S(1)} %copy-done.1, ...), custom_call_target="tpu_custom_call" | custom-call | flops 48318382080 | bytes 209715200 | tf_op jit(solution)/shard_map/gather_and_attend/pallas_call | solution.py:374
  122.9 0.0 copy-start.4
  122.9 1.6 copy-done.4
  124.6 0.0 copy-start.5
  124.6 1.4 copy-done.5
  126.0 0.0 copy-start.6
  126.0 0.9 copy-done.6
  126.9 6.7 %copy.18 = bf16[768,3072]{0,1:T(8,128)(2,1)} copy(bf16[768,3072]{1,0:T(8,128)(2,1)} %get-tuple-element.14) | data formatting | bytes 9437184
  133.6 0.0 reduce-scatter.4.cloned.1.call-update
  133.6 0.0 all-gather.2.cloned.1.call-start
  133.7 0.7 all-gather.2.cloned.1.call-update
  134.4 61.4 %reduce-scatter.4.cloned.1.call-done = bf16[384,768]{1,0:T(8,128)(2,1)} async-done(((bf16[3072,768]{1,0:T(8,128)(2,1)}), bf16[384,768]{1,0:T(8,128)(2,1)}) %reduce-scatter.4.cloned.1.call-update) | async-done | bytes 589840
  195.7 1.4 copy.19
  197.1 1.1 convert_element_type.3
  198.2 39.3 %all-gather.2.cloned.1.call-done.w_ref = bf16[768,3072]{1,0:T(8,128)(2,1)} async-done(((bf16[768,384]{1,0:T(8,128)(2,1)}), bf16[768,3072]{1,0:T(8,128)(2,1)}) %all-gather.2.cloned.1.call-update) | async-done | bytes 4718608 | tf_op jit(solution)/shard_map/all_gather | solution.py:371
  237.5 123.8 %project_and_scatter.1 = (bf16[128,3072]{1,0:T(8,128)(2,1)}, bf16[24,3,128,128]{3,2,1,0:T(8,128)(2,1)}) custom-call(bf16[6,3,512,128]{3,2,1,0:T(8,128)(2,1)} %copy-done.5, bf16[512,768]{1,0:T(8,128)(2,1)} %copy-done.6, bf16[512,3072]{1,0:T(8,128)(2,1)} %copy-done.4, bf16[768,3072]{1,0:T(8,128)(2,1)} %all-gather.2.cloned.1.call-done.w_ref, ...), custom_call_target="tpu_custom_call" | custom-call | flops 48318382080 | bytes 209715200 | tf_op jit(solution)/shard_map/project_and_scatter/pallas_call | solution.py:403
  361.3 3.1 copy.16
  364.4 0.0 copy-start.7
  364.4 2.4 copy.17
  366.8 0.0 copy-done.7
  366.8 0.9 copy.21
Async XLA Ops:
  7.2 188.6 %reduce-scatter.4.cloned.1.call-start = ((), (), s32[]{:S(2)}) async-start(), calls=%async_computation.2 | async-start | bytes 5308416
  11.5 3.1 copy-start
  11.5 3.1 copy-start.2
  11.5 3.2 copy-start.3
  14.6 1.1 copy-start.1
  122.9 1.7 copy-start.4
  124.6 1.4 copy-start.5
  126.0 0.9 copy-start.6
  133.6 103.9 %all-gather.2.cloned.1.call-start = ((), (), s32[]{:S(2)}) async-start(), calls=%async_computation.1 | async-start | bytes 5308416 | tf_op jit(solution)/shard_map/all_gather | solution.py:371
  364.4 2.4 copy-start.7
Sparse Core Ops, SparseCore 0:
  133.7 61.9 reduce-scatter.3
  197.7 39.7 all-gather.1

commit v2 on v0

v2 whole, which is shorter than its diff:
```python
import functools

import jax
import jax.numpy as jnp
from jax import lax
from jax.experimental import pallas as pl
from jax.experimental.pallas import tpu as pltpu
from jax.sharding import PartitionSpec as P

HD = 128
FRAME_TOK = 64
QUERY_TILE = 256
MESH = pl.DeviceIdType.MESH
TRANSPOSED_RHS = (((1,), (1,)), ((), ()))
TRANSPOSED_LHS = (((0,), (0,)), ((), ()))


def dot(a, b, dims=(((1,), (0,)), ((), ()))):
    return lax.dot_general(a, b, dims, preferred_element_type=jnp.float32)


def greet(devices):
    barrier = pltpu.get_barrier_semaphore()
    for device in devices:
        pl.semaphore_signal(barrier, inc=1, device_id=device, device_id_type=MESH)
    pl.semaphore_wait(barrier, len(devices))


def clip_of(frames_ref, places):
    end = 0
    which = jnp.zeros_like(places)
    for c in range(frames_ref.shape[1] - 1):
        end = end + frames_ref[0, c] * FRAME_TOK
        which = which + (places >= end).astype(jnp.int32)
    return which


def gate_rows(table_ref, steps_ref, frames_ref, start, count):
    places = start + lax.broadcasted_iota(jnp.int32, (count, 1), 0)
    which = clip_of(frames_ref, places)
    gate = table_ref[pl.ds(steps_ref[0, 0], 1), :]
    for c in range(1, steps_ref.shape[1]):
        gate = jnp.where(which >= c, table_ref[pl.ds(steps_ref[0, c], 1), :], gate)
    return gate


def probabilities(q, k, frames_ref, start, rows):
    count = q.shape[0]
    scores = dot(q, k, TRANSPOSED_RHS) * jnp.float32(HD ** -0.5)
    mine = clip_of(frames_ref, start + lax.broadcasted_iota(jnp.int32, (count, 1), 0))
    theirs = clip_of(frames_ref, lax.broadcasted_iota(jnp.int32, (1, rows), 1))
    scores = jnp.where(mine == theirs, scores, jnp.float32(-1e30))
    expo = jnp.exp(scores - jnp.max(scores, axis=-1, keepdims=True))
    return expo * (1.0 / jnp.sum(expo, axis=-1, keepdims=True))


def sublayer_kernel(
    n, n_dp, stages,
    qkv_ref, lat_ref, cot_ref, wt_ref, table_ref, steps_ref, frames_ref,
    out_ref, grads_ref, gw_ref,
    heads, attn, piece, weight, dweight, sibling, chips, part, landed, dattn, gbuf,
    own_sem, keep_sem, wo_sem, qs_sem, qr_sem, gs_sem, gr_sem,
    ws_sem, wr_sem, fs_sem, fr_sem, ps_sem, pr_sem, hs_sem, hr_sem,
    ss_sem, sr_sem, cs_sem, cr_sem,
):
    me = lax.axis_index("seq")
    dp = lax.axis_index("dp")
    core = lax.rem(dp, 2)
    chip = lax.div(dp, 2)
    n_chips = n_dp // 2
    rows, span = attn.shape
    tok, wide = out_ref.shape
    cols = wt_ref.shape[0]
    tile = min(QUERY_TILE, rows)
    chunk = span // stages
    step = 512

    def slab(block):
        return pl.ds(pl.multiple_of(block * tok, tok), tok)

    def owned(block):
        return pl.ds(pl.multiple_of(block * cols, cols), cols)

    def lanes(start):
        return pl.ds(pl.multiple_of(start, HD), chunk)

    def remote(src, dst, send, recv, device):
        return pltpu.make_async_remote_copy(
            src_ref=src, dst_ref=dst, send_sem=send, recv_sem=recv,
            device_id=device, device_id_type=MESH,
        )

    twin = (dp + 1 - 2 * core, me)

    def along(k):
        return (dp, lax.rem(me + k, n))

    def across(k):
        return (2 * lax.rem(chip + k, n_chips) + core, me)

    def block_copy(side, block):
        here = piece.at[slab(block), :]
        to = lax.rem(me + 1, n) if side == 0 else lax.rem(me + n - 1, n)
        return remote(here, here, gs_sem.at[side, block], gr_sem.at[side, block], (dp, to))

    def head_copy(k, c, source):
        peer = along(k)
        return remote(
            qkv_ref.at[:, :, lanes(peer[1] * span + c * chunk)],
            heads.at[:, slab(source), lanes(c * chunk)],
            qs_sem.at[k - 1, c], qr_sem.at[k - 1, c], peer,
        )

    def weight_copy(k, source):
        return remote(
            wt_ref, weight.at[owned(2 * source + core), :],
            ws_sem.at[k - 1], wr_sem.at[k - 1], across(k),
        )

    def weight_pass(k, source, side):
        here = weight.at[owned(2 * source + side), :]
        return remote(here, here, fs_sem.at[k], fr_sem.at[k], twin)

    def sum_copy(side, block):
        to = lax.rem(me + 1, n) if side == 0 else lax.rem(me + n - 1, n)
        return remote(
            part.at[slab(block), :], landed.at[side, block],
            ps_sem.at[side, block], pr_sem.at[side, block], (dp, to),
        )

    def grad_copy(k, c, source):
        peer = along(k)
        return remote(
            gbuf.at[:, slab(peer[1]), lanes(c * chunk)],
            grads_ref.at[:, :, lanes(source * span + c * chunk)],
            hs_sem.at[k - 1, c], hr_sem.at[k - 1, c], peer,
        )

    def grad_keep(c):
        return pltpu.make_async_copy(
            gbuf.at[:, slab(me), lanes(c * chunk)],
            grads_ref.at[:, :, lanes(me * span + c * chunk)], keep_sem.at[c],
        )

    def pair_copy(q, side):
        return remote(
            dweight.at[owned(2 * q + side), :], sibling.at[q],
            ss_sem.at[q], sr_sem.at[q], twin,
        )

    def chip_copy(k):
        return remote(
            dweight.at[owned(2 * lax.rem(chip + k, n_chips) + core), :], chips.at[k - 1],
            cs_sem.at[k - 1], cr_sem.at[k - 1], across(k),
        )

    greet(
        [along(k) for k in range(1, n)] + [across(k) for k in range(1, n_chips)] + [twin]
    )

    gate = gate_rows(table_ref, steps_ref, frames_ref, me * tok, tok)
    piece[slab(me), :] = (gate * cot_ref[...].astype(jnp.float32)).astype(jnp.bfloat16)

    @pl.when(me < n - 1)
    def _():
        block_copy(0, me).start()

    @pl.when(me > 0)
    def _():
        block_copy(1, me).start()

    def send_heads(c):
        for k in range(1, n):
            head_copy(k, c, me).start()

    send_heads(0)
    for k in range(1, n_chips):
        weight_copy(k, chip).start()
    own_weight = pltpu.make_async_copy(wt_ref, weight.at[owned(dp), :], wo_sem)
    own_weight.start()
    own = pltpu.make_async_copy(
        qkv_ref.at[:, :, pl.ds(pl.multiple_of(me * span, span), span)],
        heads.at[:, slab(me), :], own_sem,
    )
    own.start()
    own_weight.wait()
    weight_pass(0, chip, core).start()
    own.wait()

    def forward(c):
        for k in range(1, n):
            head_copy(k, c, lax.rem(me + n - k, n)).wait_recv()

        @pl.loop(0, (chunk // HD) * (rows // tile))
        def _(i):
            t, h = lax.rem(i, rows // tile), lax.div(i, rows // tile)
            here = pl.ds(pl.multiple_of(t * tile, tile), tile)
            head = pl.ds(pl.multiple_of(c * chunk + h * HD, HD), HD)
            probs = probabilities(
                heads[0, here, head], heads[1, :, head], frames_ref, t * tile, rows
            )
            mixed = dot(probs.astype(jnp.bfloat16), heads[2, :, head])
            attn[here, head] = mixed.astype(jnp.bfloat16)

    def backward(c):
        @pl.loop(0, chunk // HD)
        def _(h):
            head = pl.ds(pl.multiple_of(c * chunk + h * HD, HD), HD)
            grad_k = jnp.zeros((rows, HD), jnp.float32)
            grad_v = jnp.zeros((rows, HD), jnp.float32)
            for t in range(rows // tile):
                here = slice(t * tile, (t + 1) * tile)
                q, keys = heads[0, here, head], heads[1, :, head]
                probs = probabilities(q, keys, frames_ref, t * tile, rows)
                up = dattn[here, head]
                dprobs = dot(up, heads[2, :, head], TRANSPOSED_RHS)
                dprobs = dprobs.astype(jnp.bfloat16).astype(jnp.float32)
                dscores = probs * (dprobs - jnp.sum(probs * dprobs, axis=-1, keepdims=True))
                dscores = (dscores * jnp.float32(HD ** -0.5)).astype(jnp.bfloat16)
                gbuf[0, here, head] = dot(dscores, keys).astype(jnp.bfloat16)
                grad_k = grad_k + dot(dscores, q, TRANSPOSED_LHS)
                grad_v = grad_v + dot(probs.astype(jnp.bfloat16), up, TRANSPOSED_LHS)
            gbuf[1, :, head] = grad_k.astype(jnp.bfloat16)
            gbuf[2, :, head] = grad_v.astype(jnp.bfloat16)

        for k in range(1, n):
            grad_copy(k, c, me).start()
        grad_keep(c).start()

    def gather_hop(s):
        @pl.when(me - s >= 0)
        def _():
            block_copy(0, me - s).wait_recv()

            @pl.when(me < n - 1)
            def _():
                block_copy(0, me - s).start()

        @pl.when(me + s < n)
        def _():
            block_copy(1, me + s).wait_recv()

            @pl.when(me > 0)
            def _():
                block_copy(1, me + s).start()

    for c in range(stages):
        for s in range(1 + c * (n - 1) // stages, 1 + (c + 1) * (n - 1) // stages):
            gather_hop(s)
        if c + 1 < stages:
            send_heads(c + 1)
            forward(c)
        if c == 0:
            for k in range(1, n_chips):
                source = lax.rem(chip + n_chips - k, n_chips)
                weight_copy(k, source).wait_recv()
                weight_pass(k, source, core).start()

    for k in range(n_chips):
        weight_pass(k, lax.rem(chip + n_chips - k, n_chips), 1 - core).wait_recv()

    pair = 2 * HD if span % (2 * HD) == 0 else HD
    for c in range(0, span, pair):
        dattn[:, c:c + pair] = dot(piece[...], weight[:, c:c + pair]).astype(jnp.bfloat16)
    backward(0)
    forward(stages - 1)

    @pl.loop(0, wide // step)
    def _(i):
        here = pl.ds(pl.multiple_of(i * step, step), step)
        part[:, here] = dot(attn[...], weight[here, :], TRANSPOSED_RHS).astype(jnp.bfloat16)

    for s in range(n - 1, 0, -1):
        @pl.when((me == 0) & (me + s < n))
        def _():
            sum_copy(0, me + s).start()

        @pl.when((me == n - 1) & (me - s >= 0))
        def _():
            sum_copy(1, me - s).start()

    @pl.loop(0, wide // step)
    def _(i):
        here = pl.ds(pl.multiple_of(i * step, step), step)
        dweight[here, :] = dot(piece[:, here], attn[...], TRANSPOSED_LHS).astype(jnp.bfloat16)

    for q in range(n_chips):
        pair_copy(q, 1 - core).start()

    def add_into(target, spot, other, count):
        @pl.loop(0, count // 16)
        def _(r):
            mine = pl.ds(pl.multiple_of(spot * count + r * 16, 16), 16)
            theirs = pl.ds(pl.multiple_of(r * 16, 16), 16)
            target[mine, :] = (
                target[mine, :].astype(jnp.float32) + other[theirs, :].astype(jnp.float32)
            ).astype(jnp.bfloat16)

    def relay(side, block):
        sum_copy(side, block).wait_recv()
        add_into(part, block, landed.at[side, block], tok)
        sum_copy(side, block).start()

    for c in range(1, stages + 1):
        if c < stages:
            backward(c)
        if c == 1:
            for k in range(1, n_chips):
                q = lax.rem(chip + k, n_chips)
                pair_copy(q, core).wait_recv()
                add_into(dweight, 2 * q + core, sibling.at[q], cols)
                chip_copy(k).start()
        for s in range(1 + (c - 1) * (n - 1) // stages, 1 + c * (n - 1) // stages):
            @pl.when((n - s > me) & (me > 0))
            def _():
                relay(0, n - s)

            @pl.when((s - 1 < me) & (me < n - 1))
            def _():
                relay(1, s - 1)

    pair_copy(chip, core).wait_recv()
    total = dweight[owned(dp), :].astype(jnp.float32) + sibling[chip].astype(jnp.float32)
    for k in range(1, n_chips):
        chip_copy(k).wait_recv()
        total = total + chips[k - 1].astype(jnp.float32)
    gw_ref[...] = total

    @pl.when(me > 0)
    def _():
        sum_copy(0, me).wait_recv()

    @pl.when(me == 0)
    def _():
        landed[0, 0] = jnp.zeros_like(landed[0, 0])

    @pl.when(me < n - 1)
    def _():
        sum_copy(1, me).wait_recv()

    @pl.when(me == n - 1)
    def _():
        landed[1, n - 1] = jnp.zeros_like(landed[1, n - 1])

    gate = gate_rows(table_ref, steps_ref, frames_ref, me * tok, tok)
    proj = (
        part[slab(me), :].astype(jnp.float32)
        + landed[0, me].astype(jnp.float32)
        + landed[1, me].astype(jnp.float32)
    )
    out_ref[...] = (lat_ref[...].astype(jnp.float32) + gate * proj).astype(jnp.bfloat16)

    for s in range(n):
        @pl.when((me - s >= 0) & (me < n - 1))
        def _():
            block_copy(0, me - s).wait_send()

        @pl.when((me + s < n) & (me > 0))
        def _():
            block_copy(1, me + s).wait_send()

        if s > 0:
            @pl.when(me + s < n)
            def _():
                sum_copy(0, me + s).wait_send()

            @pl.when(me - s >= 0)
            def _():
                sum_copy(1, me - s).wait_send()

    for k in range(1, n_chips):
        weight_copy(k, chip).wait_send()
        chip_copy(k).wait_send()
    for q in range(n_chips):
        weight_pass(q, lax.rem(chip + n_chips - q, n_chips), core).wait_send()
        pair_copy(q, 1 - core).wait_send()
    for c in range(stages):
        grad_keep(c).wait()
        for k in range(1, n):
            head_copy(k, c, me).wait_send()
            grad_copy(k, c, me).wait_send()
            grad_copy(k, c, lax.rem(me + n - k, n)).wait_recv()


def body(qkv_input, latents, cotangent, out_weight, gate_table, timesteps, frames):
    tok, wide = latents.shape
    n, n_dp = lax.axis_size("seq"), lax.axis_size("dp")
    rows = tok * n
    span, cols = out_weight.shape
    stages = 3
    n_chips = n_dp // 2
    bf16 = jnp.bfloat16
    vmem = pl.BlockSpec(memory_space=pltpu.VMEM)
    smem = pl.BlockSpec(memory_space=pltpu.SMEM)
    dma = pltpu.SemaphoreType.DMA
    output, grads, grad_weight = pl.pallas_call(
        functools.partial(sublayer_kernel, n, n_dp, stages),
        out_shape=(
            jax.ShapeDtypeStruct((tok, wide), bf16),
            jax.ShapeDtypeStruct((3, tok, wide), bf16),
            jax.ShapeDtypeStruct((cols, span), jnp.float32),
        ),
        in_specs=[vmem, vmem, vmem, vmem, vmem, smem, smem],
        out_specs=(vmem, vmem, vmem),
        scratch_shapes=[
            pltpu.VMEM((3, rows, span), bf16),
            pltpu.VMEM((rows, span), bf16),
            pltpu.VMEM((rows, wide), bf16),
            pltpu.VMEM((wide, span), bf16),
            pltpu.VMEM((wide, span), bf16),
            pltpu.VMEM((n_chips, cols, span), bf16),
            pltpu.VMEM((n_chips - 1, cols, span), bf16),
            pltpu.VMEM((rows, wide), bf16),
            pltpu.VMEM((2, n, tok, wide), bf16),
            pltpu.VMEM((rows, span), bf16),
            pltpu.VMEM((3, rows, span), bf16),
            dma,
            dma((stages,)),
            dma,
            dma((n - 1, stages)),
            dma((n - 1, stages)),
            dma((2, n)),
            dma((2, n)),
            dma((n_chips - 1,)),
            dma((n_chips - 1,)),
            dma((n_chips,)),
            dma((n_chips,)),
            dma((2, n)),
            dma((2, n)),
            dma((n - 1, stages)),
            dma((n - 1, stages)),
            dma((n_chips,)),
            dma((n_chips,)),
            dma((n_chips - 1,)),
            dma((n_chips - 1,)),
        ],
        compiler_params=pltpu.CompilerParams(
            collective_id=0, has_side_effects=True, vmem_limit_bytes=60 * 2**20
        ),
        cost_estimate=pl.CostEstimate(
            flops=30 * rows * wide * span, bytes_accessed=32 * 2**20, transcendentals=0
        ),
        name="sublayer",
    )(
        qkv_input.transpose(1, 0, 2), latents, cotangent, out_weight.T,
        gate_table, timesteps, frames,
    )
    return output, grads.transpose(1, 0, 2), grad_weight.T


def solution(mesh):
    placed = (
        P(("dp", "seq"), None, None),
        P(("dp", "seq"), None),
        P(("dp", "seq"), None),
        P("seq", "dp"),
        P(),
        P("dp", None),
        P("dp", None),
    )
    return jax.shard_map(
        body,
        mesh=mesh,
        in_specs=placed,
        out_specs=(P(("dp", "seq"), None), P(("dp", "seq"), None, None), P("seq", "dp")),
        check_vma=False,
    )
```

time: 354 us -> 236 us (0.67); the launches traced: 349 us -> 236 us
  Pallas kernels: 0 us -> 227 us
  waiting for transfers between devices: 138 us -> 0 us
  blocking collectives: 77.2 us -> 0 us
  matrix products: 49.2 us -> 0 us
  local copies, waits for them, and re-layouts: 47.6 us -> 8.39 us
  other arithmetic: 17.9 us -> 0 us
  between operations: 13.9 us -> 0.65 us
  starting transfers between devices: 5.33 us -> 0 us
    pallas_call x0 -> x1, Pallas kernels: none -> 227 us  [body(): pl.pallas_call(functools.partial(sublayer_kernel, n, n_dp, stages), out_s...]
    all_to_all x1 -> x0, waiting for transfers between devices: 118 us -> none  [body(): lax.all_to_all(qkv_input, 'seq', split_axis=2, concat_axis=0, tiled=True)]
    all_to_all x1 -> x0, blocking collectives: 77.2 us -> none  [body(): lax.all_to_all(grads, 'seq', split_axis=0, concat_axis=2, tiled=True)]
    dot_general x11 -> x0, matrix products: 49.2 us -> none  [the longest x3 13.6 us: attend(): scores = jnp.einsum('qhd,khd->hqk', qf, kf) / jnp.sqrt(jnp.float32(HD))]
    all_gather x2 -> x0, waiting for transfers between devices: 19.2 us -> none  [the longest x1 19.1 us: body(): w_rows = lax.all_gather(out_weight, 'dp', axis=1, tiled=True)]
    all_to_all x4 -> x0, local copies, waits for them, and re-layouts: 14.7 us -> none  [the longest x2 9.56 us: body(): lax.all_to_all(qkv_input, 'seq', split_axis=2, concat_axis=0, tiled=True)]
    reshape x3 -> x0, local copies, waits for them, and re-layouts: 11.2 us -> none  [body(): grads = jnp.stack([grad_q, grad_k, grad_v], axis=1)]
    unnamed x27 -> x6, local copies, waits for them, and re-layouts: 18.3 us -> 8.39 us
  transfers between devices with their start and end apart: 5 -> 0, of which waited for: 2 -> 0; matrix products, arithmetic and copies ran while one was open for 19% -> 0% of each run, Pallas kernels for 0% -> 0%
where the time goes in v2:
time: 236 us
  Pallas kernels  227 us (96%)
  local copies, waits for them, and re-layouts  8.39 us (4%)
    pallas_call x1, Pallas kernels, body(): pl.pallas_call(functools.partial(sublayer_kernel, n, n_dp, stages), out_s...  227 us
    unnamed x6, local copies, waits for them, and re-layouts  8.39 us

profile of v2, /device:TPU:16, one launch (start us, length us, event | category | flops | bytes accessed | tf_op | source)
XLA Modules:
  0.0 235.8 jit_solution(5841993778136135624)
XLA Ops:
  0.6 2.1 copy.10
  2.7 226.8 %sublayer.1 = (bf16[128,3072]{1,0:T(8,128)(2,1)}, bf16[3,128,3072]{2,1,0:T(8,128)(2,1)}, f32[384,768]{1,0:T(8,128)}) custom-call(bf16[3,128,3072]{2,1,0:T(8,128)(2,1)} %bitcast.7, bf16[128,3072]{1,0:T(8,128)(2,1)} %lat_ref.1, bf16[128,3072]{1,0:T(8,128)(2,1)} %cot_ref.1, bf16[384,768]{1,0:T(8,128)(2,1)} %bitcast.6, f32[64,3072]{1,0:T(8,128)} %table_ref.1, ...), custom_call_target="tpu_custom_call" | custom-call | flops 36238786560 | bytes 33554432 | tf_op jit(solution)/shard_map/sublayer/pallas_call | solution.py:396
  229.5 0.0 copy-start
  229.5 2.8 %copy.11 = f32[768,384]{1,0:T(8,128)} copy(f32[768,384]{0,1:T(8,128)} %bitcast.5) | data formatting | bytes 2359296
  232.4 2.1 copy.14
  234.4 0.0 copy-done
  234.4 1.4 copy.15
Async XLA Ops:
  229.5 4.9 %copy-start = (bf16[3,128,3072]{2,1,0:T(8,128)(2,1)S(1)}, bf16[3,128,3072]{2,1,0:T(8,128)(2,1)}, u32[]{:S(2)}) copy-start(bf16[3,128,3072]{2,1,0:T(8,128)(2,1)} %get-tuple-element.7) | copy-start | bytes 7077892

commit v3 on v2

--- a/solution.py
+++ b/solution.py
@@ -56,10 +56,10 @@
 
 def sublayer_kernel(
     n, n_dp, stages,
-    qkv_ref, lat_ref, cot_ref, wt_ref, table_ref, steps_ref, frames_ref,
+    qkv_ref, lat_ref, cot_ref, w_ref, table_ref, steps_ref, frames_ref,
     out_ref, grads_ref, gw_ref,
     heads, attn, piece, weight, dweight, sibling, chips, part, landed, dattn, gbuf,
-    own_sem, keep_sem, wo_sem, qs_sem, qr_sem, gs_sem, gr_sem,
+    own_sem, keep_sem, qs_sem, qr_sem, gs_sem, gr_sem,
     ws_sem, wr_sem, fs_sem, fr_sem, ps_sem, pr_sem, hs_sem, hr_sem,
     ss_sem, sr_sem, cs_sem, cr_sem,
 ):
@@ -70,7 +70,7 @@
     n_chips = n_dp // 2
     rows, span = attn.shape
     tok, wide = out_ref.shape
-    cols = wt_ref.shape[0]
+    cols = wide // n_dp
     tile = min(QUERY_TILE, rows)
     chunk = span // stages
     step = 512
@@ -111,10 +111,10 @@
             qs_sem.at[k - 1, c], qr_sem.at[k - 1, c], peer,
         )
 
-    def weight_copy(k, source):
-        return remote(
-            wt_ref, weight.at[owned(2 * source + core), :],
-            ws_sem.at[k - 1], wr_sem.at[k - 1], across(k),
+    def weight_copy(k):
+        here = weight.at[owned(dp), :]
+        return remote(
+            here, here, ws_sem.at[k - 1], wr_sem.at[k - 1], across(k),
         )
 
     def weight_pass(k, source, side):
@@ -158,39 +158,39 @@
         [along(k) for k in range(1, n)] + [across(k) for k in range(1, n_chips)] + [twin]
     )
 
-    gate = gate_rows(table_ref, steps_ref, frames_ref, me * tok, tok)
-    piece[slab(me), :] = (gate * cot_ref[...].astype(jnp.float32)).astype(jnp.bfloat16)
-
-    @pl.when(me < n - 1)
-    def _():
-        block_copy(0, me).start()
-
-    @pl.when(me > 0)
-    def _():
-        block_copy(1, me).start()
-
     def send_heads(c):
         for k in range(1, n):
             head_copy(k, c, me).start()
 
-    send_heads(0)
-    for k in range(1, n_chips):
-        weight_copy(k, chip).start()
-    own_weight = pltpu.make_async_copy(wt_ref, weight.at[owned(dp), :], wo_sem)
-    own_weight.start()
+    for c in range(stages):
+        send_heads(c)
     own = pltpu.make_async_copy(
         qkv_ref.at[:, :, pl.ds(pl.multiple_of(me * span, span), span)],
         heads.at[:, slab(me), :], own_sem,
     )
     own.start()
-    own_weight.wait()
+    weight[owned(dp), :] = w_ref[...].T if w_ref.shape[0] == span else w_ref[...]
+    for k in range(1, n_chips):
+        weight_copy(k).start()
     weight_pass(0, chip, core).start()
+    gate = gate_rows(table_ref, steps_ref, frames_ref, me * tok, tok)
+    piece[slab(me), :] = (gate * cot_ref[...].astype(jnp.float32)).astype(jnp.bfloat16)
     own.wait()
 
-    def forward(c):
+    def start_gather():
+        @pl.when(me < n - 1)
+        def _():
+            block_copy(0, me).start()
+
+        @pl.when(me > 0)
+        def _():
+            block_copy(1, me).start()
+
+    def heads_landed(c):
         for k in range(1, n):
             head_copy(k, c, lax.rem(me + n - k, n)).wait_recv()
 
+    def forward(c):
         @pl.loop(0, (chunk // HD) * (rows // tile))
         def _(i):
             t, h = lax.rem(i, rows // tile), lax.div(i, rows // tile)
@@ -244,26 +244,18 @@
             def _():
                 block_copy(1, me + s).start()
 
-    for c in range(stages):
-        for s in range(1 + c * (n - 1) // stages, 1 + (c + 1) * (n - 1) // stages):
-            gather_hop(s)
-        if c + 1 < stages:
-            send_heads(c + 1)
-            forward(c)
-        if c == 0:
-            for k in range(1, n_chips):
-                source = lax.rem(chip + n_chips - k, n_chips)
-                weight_copy(k, source).wait_recv()
-                weight_pass(k, source, core).start()
-
+    heads_landed(0)
+    start_gather()
+    forward(0)
+    for k in range(1, n_chips):
+        source = lax.rem(chip + n_chips - k, n_chips)
+        weight_copy(k).wait_recv()
+        weight_pass(k, source, core).start()
+    for c in range(1, stages):
+        heads_landed(c)
+        forward(c)
     for k in range(n_chips):
         weight_pass(k, lax.rem(chip + n_chips - k, n_chips), 1 - core).wait_recv()
-
-    pair = 2 * HD if span % (2 * HD) == 0 else HD
-    for c in range(0, span, pair):
-        dattn[:, c:c + pair] = dot(piece[...], weight[:, c:c + pair]).astype(jnp.bfloat16)
-    backward(0)
-    forward(stages - 1)
 
     @pl.loop(0, wide // step)
     def _(i):
@@ -279,13 +271,12 @@
         def _():
             sum_copy(1, me - s).start()
 
-    @pl.loop(0, wide // step)
-    def _(i):
-        here = pl.ds(pl.multiple_of(i * step, step), step)
-        dweight[here, :] = dot(piece[:, here], attn[...], TRANSPOSED_LHS).astype(jnp.bfloat16)
-
-    for q in range(n_chips):
-        pair_copy(q, 1 - core).start()
+    for s in range(1, n):
+        gather_hop(s)
+
+    pair = 2 * HD if span % (2 * HD) == 0 else HD
+    for c in range(0, span, pair):
+        dattn[:, c:c + pair] = dot(piece[...], weight[:, c:c + pair]).astype(jnp.bfloat16)
 
     def add_into(target, spot, other, count):
         @pl.loop(0, count // 16)
@@ -301,30 +292,50 @@
         add_into(part, block, landed.at[side, block], tok)
         sum_copy(side, block).start()
 
-    for c in range(1, stages + 1):
-        if c < stages:
-            backward(c)
+    def relay_right(s):
+        @pl.when((n - s > me) & (me > 0))
+        def _():
+            relay(0, n - s)
+
+    def relay_left(s):
+        @pl.when((s - 1 < me) & (me < n - 1))
+        def _():
+            relay(1, s - 1)
+
+    for c in range(stages):
+        backward(c)
+        if c == 0:
+            @pl.loop(0, wide // step)
+            def _(i):
+                here = pl.ds(pl.multiple_of(i * step, step), step)
+                grown = dot(piece[:, here], attn[...], TRANSPOSED_LHS)
+                dweight[here, :] = grown.astype(jnp.bfloat16)
+
+            for q in range(n_chips):
+                pair_copy(q, 1 - core).start()
         if c == 1:
             for k in range(1, n_chips):
                 q = lax.rem(chip + k, n_chips)
                 pair_copy(q, core).wait_recv()
                 add_into(dweight, 2 * q + core, sibling.at[q], cols)
                 chip_copy(k).start()
-        for s in range(1 + (c - 1) * (n - 1) // stages, 1 + c * (n - 1) // stages):
-            @pl.when((n - s > me) & (me > 0))
-            def _():
-                relay(0, n - s)
-
-            @pl.when((s - 1 < me) & (me < n - 1))
-            def _():
-                relay(1, s - 1)
+        for s in range(1 + c * (n - 1) // stages, 1 + (c + 1) * (n - 1) // stages):
+            @pl.when(2 * me < n)
+            def _():
+                relay_right(s)
+                relay_left(s)
+
+            @pl.when(2 * me >= n)
+            def _():
+                relay_left(s)
+                relay_right(s)
 
     pair_copy(chip, core).wait_recv()
     total = dweight[owned(dp), :].astype(jnp.float32) + sibling[chip].astype(jnp.float32)
     for k in range(1, n_chips):
         chip_copy(k).wait_recv()
         total = total + chips[k - 1].astype(jnp.float32)
-    gw_ref[...] = total
+    gw_ref[...] = total.T if gw_ref.shape[0] == span else total
 
     @pl.when(me > 0)
     def _():
@@ -369,7 +380,7 @@
                 sum_copy(1, me - s).wait_send()
 
     for k in range(1, n_chips):
-        weight_copy(k, chip).wait_send()
+        weight_copy(k).wait_send()
         chip_copy(k).wait_send()
     for q in range(n_chips):
         weight_pass(q, lax.rem(chip + n_chips - q, n_chips), core).wait_send()
@@ -389,6 +400,7 @@
     span, cols = out_weight.shape
     stages = 3
     n_chips = n_dp // 2
+    turned = cols % HD != 0
     bf16 = jnp.bfloat16
     vmem = pl.BlockSpec(memory_space=pltpu.VMEM)
     smem = pl.BlockSpec(memory_space=pltpu.SMEM)
@@ -398,7 +410,7 @@
         out_shape=(
             jax.ShapeDtypeStruct((tok, wide), bf16),
             jax.ShapeDtypeStruct((3, tok, wide), bf16),
-            jax.ShapeDtypeStruct((cols, span), jnp.float32),
+            jax.ShapeDtypeStruct((cols, span) if turned else (span, cols), jnp.float32),
         ),
         in_specs=[vmem, vmem, vmem, vmem, vmem, smem, smem],
         out_specs=(vmem, vmem, vmem),
@@ -416,7 +428,6 @@
             pltpu.VMEM((3, rows, span), bf16),
             dma,
             dma((stages,)),
-            dma,
             dma((n - 1, stages)),
             dma((n - 1, stages)),
             dma((2, n)),
@@ -442,10 +453,10 @@
         ),
         name="sublayer",
     )(
-        qkv_input.transpose(1, 0, 2), latents, cotangent, out_weight.T,
-        gate_table, timesteps, frames,
-    )
-    return output, grads.transpose(1, 0, 2), grad_weight.T
+        qkv_input.transpose(1, 0, 2), latents, cotangent,
+        out_weight.T if turned else out_weight, gate_table, timesteps, frames,
+    )
+    return output, grads.transpose(1, 0, 2), grad_weight.T if turned else grad_weight
 
 
 def solution(mesh):

time: 236 us -> 194 us (0.82)
  Pallas kernels: 227 us -> 185 us
    pallas_call x1, Pallas kernels: 227 us -> 185 us  [body(): pl.pallas_call(functools.partial(sublayer_kernel, n, n_dp, stages), out_s...]
    unnamed x6 -> x5, local copies, waits for them, and re-layouts: 8.39 us -> 6.4 us
where the time goes in v3:
time: 194 us; the launch traced here: 192 us
  Pallas kernels  185 us (95%)
  local copies, waits for them, and re-layouts  6.4 us (3%)
    pallas_call x1, Pallas kernels, body(): pl.pallas_call(functools.partial(sublayer_kernel, n, n_dp, stages), out_s...  185 us
    unnamed x5, local copies, waits for them, and re-layouts  6.4 us

profile of v3, /device:TPU:16, one launch (start us, length us, event | category | flops | bytes accessed | tf_op | source)
XLA Modules:
  0.0 192.0 jit_solution(14837568992637497257)
XLA Ops:
  0.6 185.0 %sublayer.1 = (bf16[128,3072]{1,0:T(8,128)(2,1)}, bf16[3,128,3072]{2,1,0:T(8,128)(2,1)}, f32[768,384]{1,0:T(8,128)}) custom-call(bf16[3,128,3072]{2,1,0:T(8,128)(2,1)} %bitcast.3, bf16[128,3072]{1,0:T(8,128)(2,1)} %lat_ref.1, bf16[128,3072]{1,0:T(8,128)(2,1)} %cot_ref.1, bf16[768,384]{1,0:T(8,128)(2,1)} %w_ref.1, f32[64,3072]{1,0:T(8,128)} %table_ref.1, ...), custom_call_target="tpu_custom_call" | custom-call | flops 36238786560 | bytes 33554432 | tf_op jit(solution)/shard_map/sublayer/pallas_call | solution.py:408
  185.6 2.1 %copy.13 = bf16[128,3072]{1,0:T(8,128)(2,1)} copy(bf16[128,3072]{1,0:T(8,128)(2,1)} %get-tuple-element.12) | data formatting | bytes 1572864
  187.7 0.0 copy-start
  187.7 3.3 %copy.14 = bf16[128,3,3072]{2,0,1:T(8,128)(2,1)} copy(bf16[128,3,3072]{2,0,1:T(8,128)(2,1)} %bitcast.2) | data formatting | bytes 4718592
  191.0 0.0 copy-done
  191.0 1.0 copy.15
Async XLA Ops:
  187.7 3.3 %copy-start = (f32[768,384]{1,0:T(8,128)S(1)}, f32[768,384]{1,0:T(8,128)}, u32[]{:S(2)}) copy-start(f32[768,384]{1,0:T(8,128)} %get-tuple-element.14) | copy-start | bytes 3538948

commit v4 on v3

--- a/solution.py
+++ b/solution.py
@@ -227,6 +227,9 @@
             grad_copy(k, c, me).start()
         grad_keep(c).start()
 
+    def pull_back(block):
+        dattn[slab(block), :] = dot(piece[slab(block), :], weight[...]).astype(jnp.bfloat16)
+
     def gather_hop(s):
         @pl.when(me - s >= 0)
         def _():
@@ -236,6 +239,8 @@
             def _():
                 block_copy(0, me - s).start()
 
+            pull_back(me - s)
+
         @pl.when(me + s < n)
         def _():
             block_copy(1, me + s).wait_recv()
@@ -243,6 +248,8 @@
             @pl.when(me > 0)
             def _():
                 block_copy(1, me + s).start()
+
+            pull_back(me + s)
 
     heads_landed(0)
     start_gather()
@@ -271,13 +278,6 @@
         def _():
             sum_copy(1, me - s).start()
 
-    for s in range(1, n):
-        gather_hop(s)
-
-    pair = 2 * HD if span % (2 * HD) == 0 else HD
-    for c in range(0, span, pair):
-        dattn[:, c:c + pair] = dot(piece[...], weight[:, c:c + pair]).astype(jnp.bfloat16)
-
     def add_into(target, spot, other, count):
         @pl.loop(0, count // 16)
         def _(r):
@@ -302,9 +302,31 @@
         def _():
             relay(1, s - 1)
 
+    def relays(near, far):
+        @pl.when(2 * me < n)
+        def _():
+            for s in near:
+                relay_right(s)
+            for s in far:
+                relay_left(s)
+
+        @pl.when(2 * me >= n)
+        def _():
+            for s in near:
+                relay_left(s)
+            for s in far:
+                relay_right(s)
+
+    def stage_hops(c):
+        return range(1 + c * (n - 1) // stages, 1 + (c + 1) * (n - 1) // stages)
+
+    pull_back(me)
+    for s in range(1, n):
+        gather_hop(s)
+    relays(stage_hops(0), ())
     for c in range(stages):
         backward(c)
-        if c == 0:
+        if c == stages - 2:
             @pl.loop(0, wide // step)
             def _(i):
                 here = pl.ds(pl.multiple_of(i * step, step), step)
@@ -313,22 +335,13 @@
 
             for q in range(n_chips):
                 pair_copy(q, 1 - core).start()
-        if c == 1:
+        if c == stages - 1:
             for k in range(1, n_chips):
                 q = lax.rem(chip + k, n_chips)
                 pair_copy(q, core).wait_recv()
                 add_into(dweight, 2 * q + core, sibling.at[q], cols)
                 chip_copy(k).start()
-        for s in range(1 + c * (n - 1) // stages, 1 + (c + 1) * (n - 1) // stages):
-            @pl.when(2 * me < n)
-            def _():
-                relay_right(s)
-                relay_left(s)
-
-            @pl.when(2 * me >= n)
-            def _():
-                relay_left(s)
-                relay_right(s)
+        relays(stage_hops(c + 1) if c + 1 < stages else (), stage_hops(c))
 
     pair_copy(chip, core).wait_recv()
     total = dweight[owned(dp), :].astype(jnp.float32) + sibling[chip].astype(jnp.float32)

time: 194 us -> 187 us (0.964)
  Pallas kernels: 185 us -> 178 us
    pallas_call x1, Pallas kernels: 185 us -> 178 us  [body(): pl.pallas_call(functools.partial(sublayer_kernel, n, n_dp, stages), out_s...]
where the time goes in v4:
time: 187 us; the launch traced here: 185 us
  Pallas kernels  178 us (95%)
  local copies, waits for them, and re-layouts  6.4 us (3%)
    pallas_call x1, Pallas kernels, body(): pl.pallas_call(functools.partial(sublayer_kernel, n, n_dp, stages), out_s...  178 us
    unnamed x5, local copies, waits for them, and re-layouts  6.4 us

profile of v4, /device:TPU:16, one launch (start us, length us, event | category | flops | bytes accessed | tf_op | source)
XLA Modules:
  0.0 185.0 jit_solution(4241078254196590603)
XLA Ops:
  0.6 178.0 %sublayer.1 = (bf16[128,3072]{1,0:T(8,128)(2,1)}, bf16[3,128,3072]{2,1,0:T(8,128)(2,1)}, f32[768,384]{1,0:T(8,128)}) custom-call(bf16[3,128,3072]{2,1,0:T(8,128)(2,1)} %bitcast.3, bf16[128,3072]{1,0:T(8,128)(2,1)} %lat_ref.1, bf16[128,3072]{1,0:T(8,128)(2,1)} %cot_ref.1, bf16[768,384]{1,0:T(8,128)(2,1)} %w_ref.1, f32[64,3072]{1,0:T(8,128)} %table_ref.1, ...), custom_call_target="tpu_custom_call" | custom-call | flops 36238786560 | bytes 33554432 | tf_op jit(solution)/shard_map/sublayer/pallas_call | solution.py:421
  178.6 2.1 %copy.13 = bf16[128,3072]{1,0:T(8,128)(2,1)} copy(bf16[128,3072]{1,0:T(8,128)(2,1)} %get-tuple-element.12) | data formatting | bytes 1572864
  180.7 0.0 copy-start
  180.7 3.3 %copy.14 = bf16[128,3,3072]{2,0,1:T(8,128)(2,1)} copy(bf16[128,3,3072]{2,0,1:T(8,128)(2,1)} %bitcast.2) | data formatting | bytes 4718592
  184.0 0.0 copy-done
  184.0 1.0 copy.15
Async XLA Ops:
  180.7 3.3 %copy-start = (f32[768,384]{1,0:T(8,128)S(1)}, f32[768,384]{1,0:T(8,128)}, u32[]{:S(2)}) copy-start(f32[768,384]{1,0:T(8,128)} %get-tuple-element.14) | copy-start | bytes 3538948

commit v5 on v4

--- a/solution.py
+++ b/solution.py
@@ -323,7 +323,8 @@
     pull_back(me)
     for s in range(1, n):
         gather_hop(s)
-    relays(stage_hops(0), ())
+        if s == 1:
+            relays(stage_hops(0), ())
     for c in range(stages):
         backward(c)
         if c == stages - 2:
@@ -417,6 +418,7 @@
     bf16 = jnp.bfloat16
     vmem = pl.BlockSpec(memory_space=pltpu.VMEM)
     smem = pl.BlockSpec(memory_space=pltpu.SMEM)
+    anyspace = pl.BlockSpec(memory_space=pl.ANY)
     dma = pltpu.SemaphoreType.DMA
     output, grads, grad_weight = pl.pallas_call(
         functools.partial(sublayer_kernel, n, n_dp, stages),
@@ -425,8 +427,8 @@
             jax.ShapeDtypeStruct((3, tok, wide), bf16),
             jax.ShapeDtypeStruct((cols, span) if turned else (span, cols), jnp.float32),
         ),
-        in_specs=[vmem, vmem, vmem, vmem, vmem, smem, smem],
-        out_specs=(vmem, vmem, vmem),
+        in_specs=[anyspace, vmem, vmem, vmem, vmem, smem, smem],
+        out_specs=(vmem, anyspace, vmem),
         scratch_shapes=[
             pltpu.VMEM((3, rows, span), bf16),
             pltpu.VMEM((rows, span), bf16),

time: 187 us -> 186 us (level)
  no operation moved by 1% of the time
where the time goes in v5:
time: 186 us; the launch traced here: 184 us
  Pallas kernels  177 us (95%)
  local copies, waits for them, and re-layouts  6.4 us (3%)
    pallas_call x1, Pallas kernels, body(): pl.pallas_call(functools.partial(sublayer_kernel, n, n_dp, stages), out_s...  177 us
    unnamed x5, local copies, waits for them, and re-layouts  6.4 us

profile of v5, /device:TPU:16, one launch (start us, length us, event | category | flops | bytes accessed | tf_op | source)
XLA Modules:
  0.0 183.6 jit_solution(17971881609526588815)
XLA Ops:
  0.6 176.5 %sublayer.1 = (bf16[128,3072]{1,0:T(8,128)(2,1)}, bf16[3,128,3072]{2,1,0:T(8,128)(2,1)}, f32[768,384]{1,0:T(8,128)}) custom-call(bf16[3,128,3072]{2,1,0:T(8,128)(2,1)} %bitcast.3, bf16[128,3072]{1,0:T(8,128)(2,1)} %lat_ref.1, bf16[128,3072]{1,0:T(8,128)(2,1)} %cot_ref.1, bf16[768,384]{1,0:T(8,128)(2,1)} %w_ref.1, f32[64,3072]{1,0:T(8,128)} %table_ref.1, ...), custom_call_target="tpu_custom_call" | custom-call | flops 36238786560 | bytes 33554432 | tf_op jit(solution)/shard_map/sublayer/pallas_call | solution.py:423
  177.2 2.1 %copy.13 = bf16[128,3072]{1,0:T(8,128)(2,1)} copy(bf16[128,3072]{1,0:T(8,128)(2,1)} %get-tuple-element.12) | data formatting | bytes 1572864
  179.2 0.0 copy-start
  179.2 3.3 %copy.14 = bf16[128,3,3072]{2,0,1:T(8,128)(2,1)} copy(bf16[128,3,3072]{2,0,1:T(8,128)(2,1)} %bitcast.2) | data formatting | bytes 4718592
  182.6 0.0 copy-done
  182.6 1.0 copy.15
Async XLA Ops:
  179.2 3.3 %copy-start = (f32[768,384]{1,0:T(8,128)S(1)}, f32[768,384]{1,0:T(8,128)}, u32[]{:S(2)}) copy-start(f32[768,384]{1,0:T(8,128)} %get-tuple-element.14) | copy-start | bytes 3538948

commit v6 on v5

--- a/solution.py
+++ b/solution.py
@@ -405,6 +405,11 @@
             head_copy(k, c, me).wait_send()
             grad_copy(k, c, me).wait_send()
             grad_copy(k, c, lax.rem(me + n - k, n)).wait_recv()
+
+
+def store_kernel(out_in, grads_in, out_ref, grads_ref):
+    out_ref[...] = out_in[...]
+    grads_ref[...] = grads_in[...]
 
 
 def body(qkv_input, latents, cotangent, out_weight, gate_table, timesteps, frames):
@@ -471,6 +476,22 @@
         qkv_input.transpose(1, 0, 2), latents, cotangent,
         out_weight.T if turned else out_weight, gate_table, timesteps, frames,
     )
+    share = tok // 4
+    blocks = (
+        pl.BlockSpec((share, wide), lambda i: (i, 0)),
+        pl.BlockSpec((3, share, wide), lambda i: (0, i, 0)),
+    )
+    output, grads = pl.pallas_call(
+        store_kernel,
+        grid=(4,),
+        out_shape=(
+            jax.ShapeDtypeStruct(output.shape, bf16),
+            jax.ShapeDtypeStruct(grads.shape, bf16),
+        ),
+        in_specs=blocks,
+        out_specs=blocks,
+        name="store",
+    )(output, grads)
     return output, grads.transpose(1, 0, 2), grad_weight.T if turned else grad_weight
 
 

time: 186 us -> 185 us (level)
  local copies, waits for them, and re-layouts: 6.4 us -> 1.02 us
  Pallas kernels: 177 us -> 181 us
    unnamed x5 -> x3, local copies, waits for them, and re-layouts: 6.4 us -> 1.02 us
    pallas_call x0 -> x1, Pallas kernels: none -> 4.3 us  [body(): pl.pallas_call(store_kernel, grid=(4,), out_shape=(jax.ShapeDtypeStruct(o...]
where the time goes in v6:
time: 185 us; the launch traced here: 183 us
  Pallas kernels  181 us (98%)
    pallas_call x1, Pallas kernels, body(): pl.pallas_call(functools.partial(sublayer_kernel, n, n_dp, stages), out_s...  177 us
    pallas_call x1, Pallas kernels, body(): pl.pallas_call(store_kernel, grid=(4,), out_shape=(jax.ShapeDtypeStruct(o...  4.3 us

profile of v6, /device:TPU:16, one launch (start us, length us, event | category | flops | bytes accessed | tf_op | source)
XLA Modules:
  0.0 182.5 jit_solution(17259992933271799144)
XLA Ops:
  0.6 176.5 %sublayer.1 = (bf16[128,3072]{1,0:T(8,128)(2,1)}, bf16[3,128,3072]{2,1,0:T(8,128)(2,1)}, f32[768,384]{1,0:T(8,128)}) custom-call(bf16[3,128,3072]{2,1,0:T(8,128)(2,1)} %bitcast.2, bf16[128,3072]{1,0:T(8,128)(2,1)} %lat_ref.1, bf16[128,3072]{1,0:T(8,128)(2,1)} %cot_ref.1, bf16[768,384]{1,0:T(8,128)(2,1)} %w_ref.1, f32[64,3072]{1,0:T(8,128)} %table_ref.1, ...), custom_call_target="tpu_custom_call" | custom-call | flops 36238786560 | bytes 33554432 | tf_op jit(solution)/shard_map/sublayer/pallas_call | solution.py:428
  177.2 0.0 copy-start
  177.2 4.3 %store.1 = (bf16[128,3072]{1,0:T(8,128)(2,1)}, bf16[3,128,3072]{2,1,0:T(8,128)(2,1)}) custom-call(bf16[128,3072]{1,0:T(8,128)(2,1)} %get-tuple-element.8.out_in, bf16[3,128,3072]{2,1,0:T(8,128)(2,1)} %get-tuple-element.9.grads_in), custom_call_target="tpu_custom_call" | custom-call | tf_op jit(solution)/shard_map/store/pallas_call | solution.py:484
  181.5 0.0 copy-done
  181.5 1.0 copy.11
Async XLA Ops:
  177.2 4.3 %copy-start = (f32[768,384]{1,0:T(8,128)S(1)}, f32[768,384]{1,0:T(8,128)}, u32[]{:S(2)}) copy-start(f32[768,384]{1,0:T(8,128)} %get-tuple-element.18) | copy-start | bytes 3538948
